TPU v7x, 32 devices: a whole 2x2x4 slice. The times are simulated.
32 devices in a mesh: row: 8 (over y, x, core), col: 4 (over z).
Axes of the slice: x: 2, y: 2, z: 4, core: 2. Of those that a mesh axis runs over, the one named last changes fastest.
Arguments:
- features: bfloat16 [6144, 256], P(('row', 'col')), may hold values from -6 to 6
- weight: bfloat16 [256, 256], replicated, may hold values from -0.375 to 0.375
- tiles: bfloat16 [8, 4, 256, 64, 128], P('row', 'col'), may hold values from -0.0546875 to 0.0546875
- tile_rows: int32 [8, 4, 512], P('row', 'col'), may hold values from 0 to 11
- tile_cols: int32 [8, 4, 512], P('row', 'col'), may hold values from 0 to 23
- counts: int32 [8, 4], P('row', 'col'), may hold values from 128 to 512, as said below
Outputs:
- output: bfloat16 [6144, 256], P(('row', 'col'))
Inputs may be any that keep to these rules, and one draw needn't show every extreme that they name: `counts`: some grid cell has exactly 512 live slots.
All inputs are finite; a program needn't handle non-finite values.
Results may differ from a plain program's by a relative error of at most 0.0049.
Values may be sent and summed in bfloat16 or wider, within the bound.
A program may use at most 64 MiB of HBM per device.

v0:
```python
import functools

import jax
import jax.numpy as jnp
from jax import lax
from jax.experimental import pallas as pl
from jax.experimental.pallas import tpu as pltpu
from jax.sharding import PartitionSpec as P

TILE = 64
MESH = pl.DeviceIdType.MESH
CHUNKS = 8
GROUP = 8


def densify_kernel(
    counts, rows_hbm, cols_hbm, tiles_ref, dense_ref, rows, cols, tile_buf, acc, rounded,
    sems, index_sems, out_sems,
):
    pairs = tiles_ref.shape[2]
    per_chunk = pairs // CHUNKS
    index_copies = []
    for k, (src, dst) in enumerate(((rows_hbm, rows), (cols_hbm, cols))):
        copy = pltpu.make_async_copy(src, dst, index_sems.at[k])
        copy.start()
        index_copies.append(copy)
    copies = []
    for k in range(CHUNKS):
        part = pl.ds(k * per_chunk, per_chunk)
        copy = pltpu.make_async_copy(tiles_ref.at[0, 0, part], tile_buf.at[part], sems.at[k])
        copy.start()
        copies.append(copy)
    col_pairs = rounded.shape[0]
    row_tiles = rounded.shape[1] // TILE
    octets = TILE // 16
    col_octets = row_tiles * octets
    spare = 2 * col_pairs * col_octets

    @pl.loop(0, 2 * col_pairs)
    def _(i):
        zeros = jnp.zeros((col_octets, *acc.shape[1:]), acc.dtype)
        acc[pl.ds(i * col_octets, col_octets)] = zeros

    acc[spare:] = jnp.zeros((octets, *acc.shape[1:]), acc.dtype)
    for copy in index_copies:
        copy.wait()
    live = counts[0, 0]
    live_pairs = (live + 1) // 2
    low = lax.broadcasted_iota(jnp.int32, (TILE // 2, 2 * TILE), 1) < TILE

    for k in range(CHUNKS):
        copies[k].wait()
        first = k * per_chunk
        groups = jnp.clip((live_pairs - first + GROUP - 1) // GROUP, 0, per_chunk // GROUP)

        @pl.loop(0, groups)
        def _(g):
            start = first + g * GROUP
            for j in range(GROUP):
                pair = tile_buf[start + j].astype(jnp.float32)
                turned = pltpu.roll(pair, TILE, 1)
                upper, lower = slice(0, TILE // 2), slice(TILE // 2, TILE)
                even = jnp.where(low, pair[upper], turned[lower])
                odd = jnp.where(low, turned[upper], pair[lower])
                term0 = even.reshape(octets, 8, 2 * TILE)
                term1 = odd.reshape(octets, 8, 2 * TILE)
                p = 2 * (start + j)
                place0 = cols[0, 0, p] * col_octets + rows[0, 0, p] * octets
                place1 = cols[0, 0, p + 1] * col_octets + rows[0, 0, p + 1] * octets
                place0 = jnp.where(p < live, place0, spare)
                place1 = jnp.where(p + 1 < live, place1, spare)
                at0 = pl.ds(place0, octets)
                at1 = pl.ds(place1, octets)
                again = term0 * jnp.where(place0 == place1, 1.0, 0.0)
                sum0 = acc[at0] + term0
                sum1 = acc[at1] + (term1 + again)
                acc[at0] = sum0
                acc[at1] = sum1

    out_copies = []
    for i in range(col_pairs):
        even, odd = (
            acc[c * col_octets : (c + 1) * col_octets].reshape(row_tiles * TILE // 2, 2 * TILE)
            for c in (2 * i, 2 * i + 1)
        )
        left = lax.broadcasted_iota(jnp.int32, even.shape, 1) < TILE
        upper = jnp.where(left, even, pltpu.roll(odd, TILE, 1))
        lower = jnp.where(left, pltpu.roll(even, TILE, 1), odd)
        halves = [x.reshape(row_tiles, TILE // 2, 2 * TILE) for x in (upper, lower)]
        block = jnp.concatenate(halves, axis=1).reshape(rounded.shape[1:])
        rounded[i] = block.astype(rounded.dtype)
        copy = pltpu.make_async_copy(rounded.at[i], dense_ref.at[i], out_sems.at[i])
        copy.start()
        out_copies.append(copy)
    for copy in out_copies:
        copy.wait()


def densify(counts, rows, cols, tiles, row_tiles, col_tiles):
    shape = (col_tiles // 2, row_tiles * TILE, 2 * TILE)
    hbm = pl.BlockSpec(memory_space=pltpu.HBM)
    return pl.pallas_call(
        densify_kernel,
        out_shape=jax.ShapeDtypeStruct(shape, jnp.bfloat16),
        in_specs=[pl.BlockSpec(memory_space=pltpu.VMEM)] + [hbm] * 3,
        out_specs=hbm,
        scratch_shapes=[
            pltpu.SMEM(rows.shape, jnp.int32),
            pltpu.SMEM(cols.shape, jnp.int32),
            pltpu.VMEM(tiles.shape[2:], tiles.dtype),
            pltpu.VMEM((shape[0] * shape[1] // 8 + TILE // 16, 8, shape[2]), jnp.float32),
            pltpu.VMEM(shape, jnp.bfloat16),
            pltpu.SemaphoreType.DMA((CHUNKS,)),
            pltpu.SemaphoreType.DMA((2,)),
            pltpu.SemaphoreType.DMA((shape[0],)),
        ],
        compiler_params=pltpu.CompilerParams(vmem_limit_bytes=61 << 20),
        cost_estimate=pl.CostEstimate(
            flops=5_000_000_000, bytes_accessed=2 * tiles.size, transcendentals=0
        ),
    )(counts, rows, cols, tiles)


def flip(index, mask, n):
    out, bit = 0, 1
    while bit < n:
        have = (index // bit) % 2
        out = out + bit * ((1 - have) if mask & bit else have)
        bit *= 2
    return out


def combine_kernel(
    n_row, n_col, own_ref, x_ref, y_ref, across_ref, weight_ref, dense_hbm, out_ref,
    dense_ref, dense_sem, table, send, recv, gather_send, gather_recv, send_sems, recv_sems,
):
    me_row, me = lax.axis_index("row"), lax.axis_index("col")
    block = out_ref.shape[0]
    barrier = pltpu.get_barrier_semaphore()
    buddy = flip(me_row, 1, n_row)
    pl.semaphore_signal(barrier, inc=1, device_id=(buddy, me), device_id_type=MESH)
    for j in range(1, n_col):
        pl.semaphore_signal(
            barrier, inc=1, device_id=(me_row, (me + j) % n_col), device_id_type=MESH
        )
    dense_copy = pltpu.make_async_copy(dense_hbm, dense_ref, dense_sem.at[0])
    dense_copy.start()

    def rows_of(source):
        return pl.ds(pl.multiple_of(source * block, block), block)

    weight = weight_ref[...]
    sources = [flip(me_row, m, n_row) for m in (0, 2, 4, 6)]
    for source, ref in zip(sources, (own_ref, x_ref, y_ref, across_ref)):
        product = jnp.dot(ref[...], weight, preferred_element_type=jnp.float32)
        table[rows_of(source)] = product.astype(table.dtype)
    pl.semaphore_wait(barrier, n_col)

    pieces = []
    for k, source in enumerate(sources):
        part = table.at[rows_of(source)]
        copy = pltpu.make_async_remote_copy(
            src_ref=part,
            dst_ref=part,
            send_sem=gather_send.at[k],
            recv_sem=gather_recv.at[k],
            device_id=(buddy, me),
            device_id_type=MESH,
        )
        copy.start()
        pieces.append(copy)
    dense_copy.wait()
    for copy in pieces:
        copy.wait_recv()

    def partial(owner):
        at = rows_of(owner)
        left = jnp.concatenate([dense_ref[i, at] for i in range(dense_ref.shape[0])], axis=1)
        return jnp.dot(left, table[...], preferred_element_type=jnp.float32)

    copies = []
    for j in (2, 1, 3):
        peer = (me + j) % n_col
        send[j - 1] = partial(peer).astype(send.dtype)
        copy = pltpu.make_async_remote_copy(
            src_ref=send.at[j - 1],
            dst_ref=recv.at[j - 1],
            send_sem=send_sems.at[j - 1],
            recv_sem=recv_sems.at[j - 1],
            device_id=(me_row, peer),
            device_id_type=MESH,
        )
        copy.start()
        copies.append((j, copy))
    total = partial(me)
    for j, copy in copies:
        copy.wait_recv()
        total = total + recv[j - 1].astype(jnp.float32)
    out_ref[...] = jnp.maximum(total, 0.0).astype(out_ref.dtype)
    for copy in pieces:
        copy.wait_send()
    for j, copy in copies:
        copy.wait_send()


def fast_body(n_row, n_col, features, weight, tiles, tile_rows, tile_cols, counts):
    block, width = features.shape
    pieces = [features]
    for m in (2, 4, 6):
        pieces.append(lax.ppermute(features, "row", [(i, i ^ m) for i in range(n_row)]))
    dense = densify(
        counts, tile_rows, tile_cols, tiles, n_col * block // TILE, n_row * block // TILE
    )
    vmem = pl.BlockSpec(memory_space=pltpu.VMEM)
    return pl.pallas_call(
        functools.partial(combine_kernel, n_row, n_col),
        out_shape=jax.ShapeDtypeStruct((block, width), jnp.bfloat16),
        in_specs=[vmem] * 5 + [pl.BlockSpec(memory_space=pltpu.HBM)],
        out_specs=vmem,
        scratch_shapes=[
            pltpu.VMEM(dense.shape, dense.dtype),
            pltpu.SemaphoreType.DMA((1,)),
            pltpu.VMEM((n_row * block, width), jnp.bfloat16),
            pltpu.VMEM((n_col - 1, block, width), jnp.bfloat16),
            pltpu.VMEM((n_col - 1, block, width), jnp.bfloat16),
            pltpu.SemaphoreType.DMA((4,)),
            pltpu.SemaphoreType.DMA((4,)),
            pltpu.SemaphoreType.DMA((n_col - 1,)),
            pltpu.SemaphoreType.DMA((n_col - 1,)),
        ],
        compiler_params=pltpu.CompilerParams(
            collective_id=0, has_side_effects=True, vmem_limit_bytes=52 << 20
        ),
    )(*pieces, weight, dense)


def general_body(features, weight, tiles, tile_rows, tile_cols, counts):
    feature_width = weight.shape[1]
    product_rows = jnp.dot(features, weight, preferred_element_type=jnp.float32).astype(
        jnp.bfloat16
    )
    gathered = lax.all_gather(product_rows, "row", axis=0, tiled=True)
    column_table = gathered.reshape(gathered.shape[0] // TILE, TILE, feature_width)
    row_tiles = lax.axis_size("col") * features.shape[0] // TILE
    slot_count = tile_rows.shape[2]
    block_size = min(64, slot_count)
    half_block = block_size // 2
    passes = slot_count // block_size
    pair_list = tiles[0, 0]
    row_list = tile_rows[0, 0]
    col_list = tile_cols[0, 0]
    live_count = counts[0, 0]
    block_slots = jnp.arange(block_size, dtype=jnp.int32)

    def add_block(block_index, total):
        first = block_index * block_size
        pair_block = lax.dynamic_slice_in_dim(pair_list, block_index * half_block, half_block, 0)
        pair_block = pair_block.reshape(half_block, TILE, 2, TILE)
        row_block = lax.dynamic_slice_in_dim(row_list, first, block_size, 0)
        col_block = lax.dynamic_slice_in_dim(col_list, first, block_size, 0)
        picked = column_table[col_block].reshape(half_block, 2, TILE, feature_width)
        terms = jnp.einsum(
            "qajb,qjbf->qjaf", pair_block, picked, preferred_element_type=jnp.float32
        )
        terms = terms.reshape(block_size, TILE, feature_width)
        in_use = (first + block_slots < live_count).astype(jnp.float32)
        terms = terms * in_use[:, None, None]
        return total.at[row_block].add(terms)

    zero_total = jnp.zeros((row_tiles, TILE, feature_width), jnp.float32)
    total = lax.fori_loop(0, passes, add_block, zero_total)
    partial_value = total.reshape(row_tiles * TILE, feature_width)
    own_rows = lax.psum_scatter(partial_value, "col", scatter_dimension=0, tiled=True)
    return jnp.maximum(own_rows, 0.0).astype(jnp.bfloat16)


def solution(mesh):
    n_row, n_col = mesh.shape["row"], mesh.shape["col"]
    fast = (n_row, n_col) == (8, 4)
    body = functools.partial(fast_body, n_row, n_col) if fast else general_body
    return jax.shard_map(
        body,
        mesh=mesh,
        in_specs=(
            P(("row", "col"), None),
            P(),
            P("row", "col", None, None, None),
            P("row", "col", None),
            P("row", "col", None),
            P("row", "col"),
        ),
        out_specs=P(("row", "col"), None),
        check_vma=False,
    )
```

profile of v0, /device:TPU:0, one launch (start us, length us, event | category | flops | bytes accessed | tf_op | source)
XLA Modules:
  0.0 25.7 jit_solution(6593980997177615577)
XLA Ops:
  0.0 3.0 %collective-permute-start.1 = (bf16[192,256]{1,0:T(8,128)(2,1)}, bf16[192,256]{1,0:T(8,128)(2,1)S(1)}, u32[]{:S(2)}, u32[]{:S(2)}) collective-permute-start(bf16[192,256]{1,0:T(8,128)(2,1)} %own_ref.1), channel_id=1, source_target_pairs={{0,16},{4,20},{8,24},{12,28},{16,0},{20,4},{24,8},{28,12},{1,17},{... | collective-permute-start | bytes 294920 | tf_op jit(solution)/shard_map/ppermute | solution.py:210
  3.0 1.5 %collective-permute-start = (bf16[192,256]{1,0:T(8,128)(2,1)}, bf16[192,256]{1,0:T(8,128)(2,1)S(1)}, u32[]{:S(2)}, u32[]{:S(2)}) collective-permute-start(bf16[192,256]{1,0:T(8,128)(2,1)} %own_ref.1), channel_id=1, source_target_pairs={{0,8},{4,12},{8,0},{12,4},{16,24},{20,28},{24,16},{28,20},{1,9},{5... | collective-permute-start | bytes 294920 | tf_op jit(solution)/shard_map/ppermute | solution.py:210
  4.5 0.0 collective-permute-start.2
  5.1 0.0 copy-start
  5.1 0.0 copy-start.1
  5.1 4.0 %shard_map.64.dense_hbm = bf16[12,768,128]{2,1,0:T(8,128)(2,1)} custom-call(s32[1,1]{1,0:T(1,128)S(6)} %copy.8.counts, s32[1,1,512]{2,1,0:T(1,128)} %rows_hbm.1, s32[1,1,512]{2,1,0:T(1,128)} %cols_hbm.1, bf16[1,1,256,64,128]{4,3,2,1,0:T(8,128)(2,1)} %tiles_ref.1), custom_call_target="tpu_custom_call" | custom-call | flops 5000000000 | bytes 4194304 | tf_op jit(solution)/shard_map/pallas_call | solution.py:102
  9.1 0.0 collective-permute-done.1.y_ref
  9.2 0.0 collective-permute-done.x_ref
  9.2 1.0 %collective-permute-done.2.across_ref = bf16[192,256]{1,0:T(8,128)(2,1)S(1)} collective-permute-done((bf16[192,256]{1,0:T(8,128)(2,1)}, bf16[192,256]{1,0:T(8,128)(2,1)S(1)}, u32[]{:S(2)}, u32[]{:S(2)}) %collective-permute-start.2) | collective-permute-done | bytes 98336 | tf_op jit(solution)/shard_map/ppermute | solution.py:210
  10.2 0.0 copy-done
  10.2 0.0 copy-done.1
  10.2 14.8 %shard_map.65 = bf16[192,256]{1,0:T(8,128)(2,1)S(1)} custom-call(bf16[192,256]{1,0:T(8,128)(2,1)S(1)} %copy-done.1, bf16[192,256]{1,0:T(8,128)(2,1)S(1)} %collective-permute-done.x_ref, bf16[192,256]{1,0:T(8,128)(2,1)S(1)} %collective-permute-done.1.y_ref, bf16[192,256]{1,0:T(8,128)(2,1)S(1)} %collective-permute-done.2.across_ref, ...), custom_call_target="tpu_custom_call" | custom-call | tf_op jit(solution)/shard_map/pallas_call | solution.py:215
  25.0 0.6 %copy.9 = bf16[192,256]{1,0:T(8,128)(2,1)} copy(bf16[192,256]{1,0:T(8,128)(2,1)S(1)} %shard_map.65) | data formatting | bytes 196608
Async XLA Ops:
  0.0 9.1 %collective-permute-start.1 = (bf16[192,256]{1,0:T(8,128)(2,1)}, bf16[192,256]{1,0:T(8,128)(2,1)S(1)}, u32[]{:S(2)}, u32[]{:S(2)}) collective-permute-start(bf16[192,256]{1,0:T(8,128)(2,1)} %own_ref.1), channel_id=1, source_target_pairs={{0,16},{4,20},{8,24},{12,28},{16,0},{20,4},{24,8},{28,12},{1,17},{... | collective-permute-start | bytes 294920 | tf_op jit(solution)/shard_map/ppermute | solution.py:210
  3.0 6.2 %collective-permute-start = (bf16[192,256]{1,0:T(8,128)(2,1)}, bf16[192,256]{1,0:T(8,128)(2,1)S(1)}, u32[]{:S(2)}, u32[]{:S(2)}) collective-permute-start(bf16[192,256]{1,0:T(8,128)(2,1)} %own_ref.1), channel_id=1, source_target_pairs={{0,8},{4,12},{8,0},{12,4},{16,24},{20,28},{24,16},{28,20},{1,9},{5... | collective-permute-start | bytes 294920 | tf_op jit(solution)/shard_map/ppermute | solution.py:210
  4.5 5.7 %collective-permute-start.2 = (bf16[192,256]{1,0:T(8,128)(2,1)}, bf16[192,256]{1,0:T(8,128)(2,1)S(1)}, u32[]{:S(2)}, u32[]{:S(2)}) collective-permute-start(bf16[192,256]{1,0:T(8,128)(2,1)} %own_ref.1), channel_id=1, source_target_pairs={{0,24},{4,28},{8,16},{12,20},{16,8},{20,12},{24,0},{28,4},{1,25},{... | collective-permute-start | bytes 294920 | tf_op jit(solution)/shard_map/ppermute | solution.py:210
  5.1 5.1 %copy-start = (bf16[256,256]{1,0:T(8,128)(2,1)S(1)}, bf16[256,256]{1,0:T(8,128)(2,1)}, u32[]{:S(2)}) copy-start(bf16[256,256]{1,0:T(8,128)(2,1)} %weight_ref.1) | copy-start | bytes 393220
  5.1 5.1 %copy-start.1 = (bf16[192,256]{1,0:T(8,128)(2,1)S(1)}, bf16[192,256]{1,0:T(8,128)(2,1)}, u32[]{:S(2)}) copy-start(bf16[192,256]{1,0:T(8,128)(2,1)} %own_ref.1) | copy-start | bytes 294916
where the time goes:
time: 25.9 us; the launch traced here: 25.7 us
  Pallas kernels  18.8 us (73%)
  starting transfers between devices  4.46 us (17%)
  waiting for transfers between devices  1.03 us (4%)
  between operations  0.7 us (3%)
  local copies, waits for them, and re-layouts  0.65 us (3%)
    pallas_call x1, Pallas kernels, fast_body(): pl.pallas_call(functools.partial(combine_kernel, n_row, n_col), out_shape...  14.8 us
    ppermute x3, starting transfers between devices, fast_body(): lax.ppermute(features, 'row', [(i, i ^ m) for i in range(n_row)])  4.46 us
    pallas_call x1, Pallas kernels, densify(): pl.pallas_call(densify_kernel, out_shape=jax.ShapeDtypeStruct(shape, jnp....  4 us
    ppermute x3, waiting for transfers between devices, fast_body(): lax.ppermute(features, 'row', [(i, i ^ m) for i in range(n_row)])  1.03 us
    unnamed x5, local copies, waits for them, and re-layouts  0.65 us
  transfers between devices with their start and end apart: 3, of which 1 were waited for; matrix products, arithmetic and copies ran while one was open for 0% of the time, Pallas kernels for 16%

commit v1 on v0

--- a/solution.py
+++ b/solution.py
@@ -14,7 +14,7 @@
 
 
 def densify_kernel(
-    counts, rows_hbm, cols_hbm, tiles_ref, dense_ref, rows, cols, tile_buf, acc, rounded,
+    counts, rows_hbm, cols_hbm, tiles_ref, dense_ref, rows, cols, tile_buf, acc, odd_acc, rounded,
     sems, index_sems, out_sems,
 ):
     pairs = tiles_ref.shape[2]
@@ -40,8 +40,10 @@
     def _(i):
         zeros = jnp.zeros((col_octets, *acc.shape[1:]), acc.dtype)
         acc[pl.ds(i * col_octets, col_octets)] = zeros
+        odd_acc[pl.ds(i * col_octets, col_octets)] = zeros
 
     acc[spare:] = jnp.zeros((octets, *acc.shape[1:]), acc.dtype)
+    odd_acc[spare:] = jnp.zeros((octets, *acc.shape[1:]), acc.dtype)
     for copy in index_copies:
         copy.wait()
     live = counts[0, 0]
@@ -71,16 +73,16 @@
                 place1 = jnp.where(p + 1 < live, place1, spare)
                 at0 = pl.ds(place0, octets)
                 at1 = pl.ds(place1, octets)
-                again = term0 * jnp.where(place0 == place1, 1.0, 0.0)
-                sum0 = acc[at0] + term0
-                sum1 = acc[at1] + (term1 + again)
-                acc[at0] = sum0
-                acc[at1] = sum1
+                acc[at0] += term0
+                odd_acc[at1] += term1
 
     out_copies = []
     for i in range(col_pairs):
         even, odd = (
-            acc[c * col_octets : (c + 1) * col_octets].reshape(row_tiles * TILE // 2, 2 * TILE)
+            (
+                acc[c * col_octets : (c + 1) * col_octets]
+                + odd_acc[c * col_octets : (c + 1) * col_octets]
+            ).reshape(row_tiles * TILE // 2, 2 * TILE)
             for c in (2 * i, 2 * i + 1)
         )
         left = lax.broadcasted_iota(jnp.int32, even.shape, 1) < TILE
@@ -108,6 +110,7 @@
             pltpu.SMEM(rows.shape, jnp.int32),
             pltpu.SMEM(cols.shape, jnp.int32),
             pltpu.VMEM(tiles.shape[2:], tiles.dtype),
+            pltpu.VMEM((shape[0] * shape[1] // 8 + TILE // 16, 8, shape[2]), jnp.float32),
             pltpu.VMEM((shape[0] * shape[1] // 8 + TILE // 16, 8, shape[2]), jnp.float32),
             pltpu.VMEM(shape, jnp.bfloat16),
             pltpu.SemaphoreType.DMA((CHUNKS,)),

time: 25.9 us -> 25.6 us (0.988)
  the two profiles are of different devices: /device:TPU:0 before, /device:TPU:1 now
where the time goes in v1:
time: 25.6 us; the launch traced here: 25.2 us
  Pallas kernels  20.5 us (80%)
  starting transfers between devices  3.28 us (13%)
  between operations  0.73 us (3%)
  local copies, waits for them, and re-layouts  0.65 us (3%)
    pallas_call x1, Pallas kernels, fast_body(): pl.pallas_call(functools.partial(combine_kernel, n_row, n_col), out_shape...  14.1 us
    pallas_call x1, Pallas kernels, densify(): pl.pallas_call(densify_kernel, out_shape=jax.ShapeDtypeStruct(shape, jnp....  6.4 us
    ppermute x3, starting transfers between devices, fast_body(): lax.ppermute(features, 'row', [(i, i ^ m) for i in range(n_row)])  3.28 us
    unnamed x5, local copies, waits for them, and re-layouts  0.65 us
  transfers between devices with their start and end apart: 3, of which 0 were waited for; matrix products, arithmetic and copies ran while one was open for 0% of the time, Pallas kernels for 25%

profile of v1, /device:TPU:1, one launch (start us, length us, event | category | flops | bytes accessed | tf_op | source)
XLA Modules:
  0.0 25.2 jit_solution(5144564952181441566)
XLA Ops:
  0.0 2.1 %collective-permute-start.1 = (bf16[192,256]{1,0:T(8,128)(2,1)}, bf16[192,256]{1,0:T(8,128)(2,1)S(1)}, u32[]{:S(2)}, u32[]{:S(2)}) collective-permute-start(bf16[192,256]{1,0:T(8,128)(2,1)} %own_ref.1), channel_id=1, source_target_pairs={{0,16},{4,20},{8,24},{12,28},{16,0},{20,4},{24,8},{28,12},{1,17},{... | collective-permute-start | bytes 294920 | tf_op jit(solution)/shard_map/ppermute | solution.py:213
  2.1 1.2 %collective-permute-start = (bf16[192,256]{1,0:T(8,128)(2,1)}, bf16[192,256]{1,0:T(8,128)(2,1)S(1)}, u32[]{:S(2)}, u32[]{:S(2)}) collective-permute-start(bf16[192,256]{1,0:T(8,128)(2,1)} %own_ref.1), channel_id=1, source_target_pairs={{0,8},{4,12},{8,0},{12,4},{16,24},{20,28},{24,16},{28,20},{1,9},{5... | collective-permute-start | bytes 294920 | tf_op jit(solution)/shard_map/ppermute | solution.py:213
  3.3 0.0 collective-permute-start.2
  3.9 0.0 copy-start
  3.9 0.0 copy-start.1
  4.0 6.4 %shard_map.64.dense_hbm = bf16[12,768,128]{2,1,0:T(8,128)(2,1)} custom-call(s32[1,1]{1,0:T(1,128)S(6)} %copy.8.counts, s32[1,1,512]{2,1,0:T(1,128)} %rows_hbm.1, s32[1,1,512]{2,1,0:T(1,128)} %cols_hbm.1, bf16[1,1,256,64,128]{4,3,2,1,0:T(8,128)(2,1)} %tiles_ref.1), custom_call_target="tpu_custom_call" | custom-call | flops 5000000000 | bytes 4194304 | tf_op jit(solution)/shard_map/pallas_call | solution.py:104
  10.4 0.0 collective-permute-done.1.y_ref
  10.4 0.0 collective-permute-done.x_ref
  10.4 0.0 collective-permute-done.2.across_ref
  10.4 0.0 copy-done
  10.4 0.0 copy-done.1
  10.4 14.1 %shard_map.65 = bf16[192,256]{1,0:T(8,128)(2,1)S(1)} custom-call(bf16[192,256]{1,0:T(8,128)(2,1)S(1)} %copy-done.1, bf16[192,256]{1,0:T(8,128)(2,1)S(1)} %collective-permute-done.x_ref, bf16[192,256]{1,0:T(8,128)(2,1)S(1)} %collective-permute-done.1.y_ref, bf16[192,256]{1,0:T(8,128)(2,1)S(1)} %collective-permute-done.2.across_ref, ...), custom_call_target="tpu_custom_call" | custom-call | tf_op jit(solution)/shard_map/pallas_call | solution.py:218
  24.5 0.6 %copy.9 = bf16[192,256]{1,0:T(8,128)(2,1)} copy(bf16[192,256]{1,0:T(8,128)(2,1)S(1)} %shard_map.65) | data formatting | bytes 196608
Async XLA Ops:
  0.0 10.4 %collective-permute-start.1 = (bf16[192,256]{1,0:T(8,128)(2,1)}, bf16[192,256]{1,0:T(8,128)(2,1)S(1)}, u32[]{:S(2)}, u32[]{:S(2)}) collective-permute-start(bf16[192,256]{1,0:T(8,128)(2,1)} %own_ref.1), channel_id=1, source_target_pairs={{0,16},{4,20},{8,24},{12,28},{16,0},{20,4},{24,8},{28,12},{1,17},{... | collective-permute-start | bytes 294920 | tf_op jit(solution)/shard_map/ppermute | solution.py:213
  2.1 8.3 %collective-permute-start = (bf16[192,256]{1,0:T(8,128)(2,1)}, bf16[192,256]{1,0:T(8,128)(2,1)S(1)}, u32[]{:S(2)}, u32[]{:S(2)}) collective-permute-start(bf16[192,256]{1,0:T(8,128)(2,1)} %own_ref.1), channel_id=1, source_target_pairs={{0,8},{4,12},{8,0},{12,4},{16,24},{20,28},{24,16},{28,20},{1,9},{5... | collective-permute-start | bytes 294920 | tf_op jit(solution)/shard_map/ppermute | solution.py:213
  3.3 7.1 %collective-permute-start.2 = (bf16[192,256]{1,0:T(8,128)(2,1)}, bf16[192,256]{1,0:T(8,128)(2,1)S(1)}, u32[]{:S(2)}, u32[]{:S(2)}) collective-permute-start(bf16[192,256]{1,0:T(8,128)(2,1)} %own_ref.1), channel_id=1, source_target_pairs={{0,24},{4,28},{8,16},{12,20},{16,8},{20,12},{24,0},{28,4},{1,25},{... | collective-permute-start | bytes 294920 | tf_op jit(solution)/shard_map/ppermute | solution.py:213
  3.9 6.5 %copy-start = (bf16[256,256]{1,0:T(8,128)(2,1)S(1)}, bf16[256,256]{1,0:T(8,128)(2,1)}, u32[]{:S(2)}) copy-start(bf16[256,256]{1,0:T(8,128)(2,1)} %weight_ref.1) | copy-start | bytes 393220
  3.9 6.5 %copy-start.1 = (bf16[192,256]{1,0:T(8,128)(2,1)S(1)}, bf16[192,256]{1,0:T(8,128)(2,1)}, u32[]{:S(2)}) copy-start(bf16[192,256]{1,0:T(8,128)(2,1)} %own_ref.1) | copy-start | bytes 294916
